TPU v7x, 32 devices: a whole 2x2x4 slice. The times are simulated.
32 devices in a mesh: wall: 4 (over z), span: 8 (over y, x, core).
Axes of the slice: x: 2, y: 2, z: 4, core: 2. Of those that a mesh axis runs over, the one named last changes fastest.
Arguments:
- velocity: float32 [3, 4, 1024, 1024], P(None, None, 'wall', 'span'), may hold values from -6 to 6
- lower_weight: float32 [4, 1024, 1024], P(None, 'wall', 'span'), may hold values from 1000 to 100000
- upper_weight: float32 [4, 1024, 1024], P(None, 'wall', 'span'), may hold values from 1000 to 100000
- forces: float32 [3, 4, 8, 8, 4, 768], P(None, 'wall', 'span'), may hold values from -6 to 6
- cells: int32 [4, 8, 8, 4, 768], P('wall', 'span'), may hold values from 0 to 32767
- counts: int32 [4, 8, 8, 4], P('wall', 'span'), may hold values from 1 to 768, as said below
Outputs:
- velocity_next: float32 [3, 4, 1024, 1024], P(None, None, 'wall', 'span')
- deposit: bfloat16 [3, 4, 1024, 1024], P(None, None, 'wall', 'span')
Inputs may be any that keep to these rules, and one draw needn't show every extreme that they name: `counts`: in every wall row one destination receives 768 live slots from every sender in one plane.
All inputs are finite; a program needn't handle non-finite values.
Results may differ from a plain program's by a relative error of at most 0.0024.
Values sent between devices are 32-bit elements; how exact they have to be, the bound alone decides.
No kernel may reach another device: no remote copies, remote signals or barrier semaphores. Data moves between devices by JAX's collectives and lax.ppermute only.
A program may use at most 64 MiB of HBM per device.

v0:
```python
import jax
import jax.numpy as jnp
from jax import lax
from jax.experimental import pallas as pl
from jax.experimental.pallas import tpu as pltpu
from jax.sharding import PartitionSpec as P

diffusion_number = 0.2
segments = 8
lanes = 128
group = 4
count_bits, plane_bit = 10, 24
in_vmem = pl.BlockSpec(memory_space=pltpu.VMEM)
in_smem = pl.BlockSpec(memory_space=pltpu.SMEM)
in_hbm = pl.BlockSpec(memory_space=pltpu.HBM)


def call(body, out_shape, out_specs, in_specs, scratch, mebibytes, flops):
    return pl.pallas_call(
        body,
        out_shape=out_shape,
        in_specs=in_specs,
        out_specs=out_specs,
        scratch_shapes=scratch,
        compiler_params=pltpu.CompilerParams(vmem_limit_bytes=mebibytes << 20),
        cost_estimate=pl.CostEstimate(flops=flops, bytes_accessed=4 << 20, transcendentals=0),
    )


def f32(*shape):
    return jax.ShapeDtypeStruct(shape, jnp.float32)


def scratch(*shape):
    return pltpu.VMEM(shape, jnp.float32)


def lane_iota(shape):
    return lax.broadcasted_iota(jnp.int32, shape, len(shape) - 1)


def reciprocal(value):
    rough = pl.reciprocal(value, approx=True)
    return rough * (2.0 - value * rough)


def start_all(copies):
    for copy in copies:
        copy.start()


def wait_all(copies):
    for copy in copies:
        copy.wait()


def copies_of(sources, targets, sems, first=0):
    return [
        pltpu.make_async_copy(source, target, sems.at[first + n])
        for n, (source, target) in enumerate(zip(sources, targets))
    ]


def pack_kernel(velocity_hbm, forces_hbm, send_hbm, velocity, forces, send, columns, turned, sems):
    components, planes, height, across = velocity_hbm.shape
    receivers, capacity = forces_hbm.shape[1], forces_hbm.shape[3]
    chunks = capacity // lanes
    lines = components * planes
    parts = height // lanes
    slot = components + 1
    copies = copies_of(
        [forces_hbm.at[c] for c in range(components)],
        [forces.at[c] for c in range(components)],
        sems,
    )
    places = [(c, x) for c in range(components) for x in range(planes)]
    copies += copies_of(
        [velocity_hbm.at[here] for here in places],
        [velocity.at[here] for here in places],
        sems,
        components,
    )
    start_all(copies)
    me = lax.axis_index("span")
    wait_all(copies[:components])
    outgoing = []
    for d in range(receivers):
        owner = lax.rem(me + d, receivers)
        for c in range(components):
            for k in range(chunks):
                value = forces[c, owner, :, k * lanes : (k + 1) * lanes]
                send[owner, pl.ds(k * slot + c, planes, stride=chunks * slot), :] = value
        index = components + lines + d
        copy = pltpu.make_async_copy(send.at[owner], send_hbm.at[owner], sems.at[index])
        outgoing.append(copy)
        if d not in (1, receivers - 1):
            copy.start()
    lane = lane_iota((height, across))
    picked = jnp.zeros((height, across), jnp.float32)
    for k in range(lines):
        copies[components + k].wait()
        rolled = pltpu.roll(velocity[k // planes, k % planes], 2 * k + 1, 1)
        picked = jnp.where((lane >> 1) == k, rolled, picked)
    columns[...] = picked
    below = lax.rem(me + receivers - 1, receivers)
    above = lax.rem(me + 1, receivers)
    for p in range(parts):
        turned[p] = columns[p * lanes : (p + 1) * lanes, :].T
        target = pl.ds(p * slot + components, lines, stride=parts * slot)
        send[below, target, :] = turned[p, pl.ds(1, lines, stride=2), :]
        send[above, target, :] = turned[p, pl.ds(0, lines, stride=2), :]
    outgoing[1].start()
    outgoing[receivers - 1].start()
    wait_all(outgoing)


def prepare_kernel(counts, cells_hbm, velocity, lower, upper, *refs):
    (rhs, inv, first, inner, ends, coefs, cell_rows, work) = refs[8:16]
    (cells, inv_b, gain_b, rows, sems) = refs[16:]
    outgoing = copies_of(refs[8:16], refs[:8], sems)
    cells_copy = pltpu.make_async_copy(cells_hbm, cells, sems.at[8])
    cells_copy.start()
    components, planes, height, across = velocity.shape
    steps = inv.shape[0] + 1
    last = steps - 1
    rest = height - segments * steps
    knots = segments + rest
    senders, capacity = cells.shape[0], cells.shape[2]
    chunks = capacity // lanes
    pairs = planes * senders
    pairs_each = -(-pairs // last)

    def list_pair(i, n):
        used = jnp.minimum(i, pairs - 1)
        x = lax.div(used, senders)
        s = used - x * senders
        count = jnp.where(i < pairs, counts[x, s], 0)
        base = (x << plane_bit) + (((s * planes + x) * chunks) << count_bits)
        for k in range(chunks):
            live = jnp.maximum(count - k * lanes, 0)
            work[group + n + k] = base + (k << count_bits) + live
        n = n + lax.div(count + lanes - 1, lanes)
        for extra in range(group):
            work[group + n + extra] = 0
        return jnp.where(s == senders - 1, lax.div(n + group - 1, group) * group, n)

    def of_step(ref, t):
        return ref[:, pl.ds(t, segments, stride=steps), :]

    one = jnp.ones((planes, segments, across), jnp.float32)
    zero = jnp.zeros_like(one)
    size = 8
    lane = lane_iota((size, across))

    def stencil(n):
        part = pl.ds(pl.multiple_of(n * size, size), size)
        for c in range(components):
            values = [velocity[c, x, part, :] for x in range(planes)]
            for x in range(planes):
                v = values[x]
                around = values[(x - 1) % planes] + values[(x + 1) % planes]
                around = around + jnp.where(lane == 0, 0.0, pltpu.roll(v, 1, 1))
                around = around + jnp.where(lane == across - 1, 0.0, pltpu.roll(v, across - 1, 1))
                rhs[c, x, part, :] = (1.0 - 4.0 * diffusion_number) * v + diffusion_number * around

    def factor(t, carry):
        d, d_b, low_gain, high_gain, sum_last, sum_first, n = carry
        low, up = of_step(lower, t), of_step(upper, t)
        e = 1.0 + low * d
        inverse = reciprocal(up + e)
        g = low * inverse
        inv[t] = inverse
        back = last - 1 - t
        low_b, up_b = of_step(lower, back), of_step(upper, back)
        e_b = 1.0 + up_b * d_b
        inverse_b = reciprocal(low_b + e_b)
        g_b = up_b * inverse_b
        inv_b[back] = inverse_b
        gain_b[back] = g_b
        stencil(t)
        for extra in range(pairs_each):
            n = list_pair(t * pairs_each + extra, n)
        return (
            e * inverse,
            e_b * inverse_b,
            low_gain * g,
            high_gain * g_b,
            inverse + g * sum_last,
            inverse_b + g_b * sum_first,
            n,
        )

    carry = lax.fori_loop(0, last, factor, (one, one, one, one, zero, zero, 0))
    _, _, low_gain, high_gain, sum_last, sum_first, total = carry
    for extra in range(2 * group):
        work[group + total + extra] = (planes - 1) << plane_bit
    work[0] = lax.div(total + 2 * group - 1, 2 * group)
    for n in range(last, height // size):
        stencil(n)
    start_all([outgoing[7], outgoing[0], outgoing[1]])
    cells_copy.wait()

    def one_sender(s, carry):
        for k in range(chunks):
            start = s * planes * chunks + k
            value = cells[s, :, k * lanes : (k + 1) * lanes]
            cell_rows[pl.ds(start, planes, stride=chunks), :] = value
        return carry

    lax.fori_loop(0, senders, one_sender, 0, unroll=4)
    outgoing[6].start()

    def weigh(t, q):
        first[t] = inv_b[t] * q
        return q * gain_b[t]

    lax.fori_loop(0, last, weigh, one, unroll=6)
    outgoing[2].start()

    low_sep, up_sep = of_step(lower, last), of_step(upper, last)
    segment = lax.broadcasted_iota(jnp.int32, one.shape, 1)
    is_end = segment == segments - 1
    above = jnp.where(is_end, 0.0, jnp.roll(sum_first, -1, axis=1))
    couple_high = up_sep * jnp.where(is_end, 1.0, jnp.roll(high_gain, -1, axis=1))
    killing = 1.0 + low_sep * sum_last + up_sep * above
    ends[2, :, :segments, :] = low_sep
    ends[3, :, :segments, :] = up_sep
    tail = slice(height - rest, height)
    low_rest, up_rest = lower[:, tail, :], upper[:, tail, :]
    for n, (value, other) in enumerate(
        (
            (low_sep * low_gain, low_rest),
            (couple_high, up_rest),
            (killing, jnp.ones_like(low_rest)),
        )
    ):
        for x in range(planes):
            rows[n, x * knots : x * knots + segments, :] = value[x]
            rows[n, x * knots + segments : (x + 1) * knots, :] = other[x]
    for x in range(planes):
        rows[3, x * knots : x * knots + segments, :] = high_gain[x]
        rows[4, x * knots : x * knots + segments, :] = sum_first[x]

    def row(n, s):
        return rows[n, pl.ds(s, planes, stride=knots), :]

    top = knots - 1
    one_row = jnp.ones((planes, across), jnp.float32)
    d, d_b = one_row, one_row
    inv_s, gain_s, ratio_s = [], [], []
    inv_sb, gain_sb = [None] * top, [None] * top
    for s in range(top):
        e = row(2, s) + row(0, s) * d
        inverse = reciprocal(row(1, s) + e)
        inv_s.append(inverse)
        gain_s.append(row(0, s) * inverse)
        ratio_s.append(row(1, s) * inverse)
        d = e * inverse
        back = top - 1 - s
        e_b = row(2, back) + row(1, back) * d_b
        inverse_b = reciprocal(row(0, back) + e_b)
        inv_sb[back] = inverse_b
        gain_sb[back] = row(1, back) * inverse_b
        d_b = e_b * inverse_b
        inner[0, s] = inv_s[s]
        inner[1, s] = gain_s[s]
        inner[2, s] = ratio_s[s]
    outgoing[3].start()
    run = row(0, top)
    low_total = one_row
    sum_top = one_row
    rows[5, pl.ds(top, planes, stride=knots), :] = one_row
    for s in reversed(range(top)):
        weight = run * inv_s[s]
        rows[5, pl.ds(s, planes, stride=knots), :] = weight
        sum_top = sum_top + weight * row(2, s)
        run = run * gain_s[s]
        low_total = low_total * gain_s[s]
    run = row(3, 0)
    high_total = one_row
    sum_bottom = row(4, 0)
    rows[6, pl.ds(top, planes, stride=knots), :] = jnp.zeros_like(one_row)
    for s in range(top):
        weight = run * inv_sb[s]
        rows[6, pl.ds(s, planes, stride=knots), :] = weight
        sum_bottom = sum_bottom + weight * row(2, s)
        run = run * gain_sb[s]
        high_total = high_total * ratio_s[s]
    coef = (
        row(0, top) * low_total,
        sum_top,
        row(1, top),
        sum_bottom,
        row(3, 0) * high_total,
    )
    for n, value in enumerate(coef):
        coefs[n * planes : (n + 1) * planes, :] = value
    for n in range(2):
        for x in range(planes):
            ends[n, x] = rows[5 + n, x * knots : (x + 1) * knots, :]
    start_all(outgoing[4:6])
    wait_all(outgoing)


def deposit_kernel(got, *refs):
    (deposit_hbm, swept, prefix, reduced, sums) = refs[8:13]
    (work, cell_rows, rhs, inv, first, ends, coefs, lower) = refs[13:21]
    (field, total, lefts, rights, columns, edges, in_sems, sems) = refs[21:]
    incoming = copies_of(refs[:8], refs[13:21], in_sems)
    start_all(incoming)
    components, planes, height, across = rhs.shape
    steps = inv.shape[0] + 1
    last = steps - 1
    knots = ends.shape[2]
    rest = knots - segments
    slot = components + 1
    senders = lax.axis_size("span")
    block = got.shape[0] // senders
    parts = height // lanes
    shift = across.bit_length() - 1
    lines = components * planes
    kind = jnp.bfloat16 if max(height, across) <= 256 else jnp.float32

    me = lax.axis_index("span")
    below = lax.rem(me + senders - 1, senders)
    above = lax.rem(me + 1, senders)
    total[...] = jnp.zeros_like(total)
    for p in range(parts):
        for n, owner in enumerate((above, below)):
            start = owner * block + p * slot + components
            columns[p, pl.ds(n, lines, stride=2), :] = got[pl.ds(start, lines, stride=parts * slot), :]
        edges[p * lanes : (p + 1) * lanes, :] = diffusion_number * columns[p].T

    tile = 16
    base = lax.broadcasted_iota(jnp.int32, (tile, lanes), 0)
    height_ids = [(base + n * tile).astype(jnp.float32).astype(kind) for n in range(height // tile)]
    across_ids = height_ids[: across // tile]
    lane = lane_iota((1, lanes))
    one = jnp.ones((tile, lanes), jnp.bfloat16)
    none = jnp.zeros((tile, lanes), jnp.bfloat16)

    def spread(row, to):
        return jnp.broadcast_to(row, (tile, lanes)).astype(to)

    def build(n, half):
        for g in range(group):
            word = work[(n + 1) * group + g]
            ident = (word >> count_bits) & ((1 << (plane_bit - count_bits)) - 1)
            live = word & ((1 << count_bits) - 1)
            there = slice(g * lanes, (g + 1) * lanes)
            cell = cell_rows[pl.ds(ident, 1), :]
            up = jnp.where(lane < live, cell >> shift, -1).astype(jnp.float32)
            side = (cell & (across - 1)).astype(jnp.float32)
            up, side = spread(up, kind), spread(side, kind)
            for i, ids in enumerate(height_ids):
                lefts[half][i * tile : (i + 1) * tile, there] = jnp.where(up == ids, one, none)
            masks = [side == ids for ids in across_ids]
            for c in range(components):
                force = got[pl.ds(ident * slot + c, 1), :]
                rest_of = force - force.astype(jnp.bfloat16).astype(jnp.float32)
                for m, value in enumerate((force, rest_of)):
                    value = spread(value, jnp.bfloat16)
                    start = (m * components + c) * across
                    for i, mask in enumerate(masks):
                        place = slice(start + i * tile, start + (i + 1) * tile)
                        rights[half][place, there] = jnp.where(mask, value, none)

    def add(n, half):
        total[work[(n + 1) * group] >> plane_bit] += lax.dot_general(
            rights[half][...],
            lefts[half][...],
            (((1,), (1,)), ((), ())),
            preferred_element_type=jnp.float32,
        )

    def two_steps(n, carry):
        build(2 * n + 1, 1)
        add(2 * n, 0)
        build(2 * n + 2, 0)
        add(2 * n + 1, 1)
        return carry

    wait_all(incoming[:2])
    build(0, 0)
    lax.fori_loop(0, work[0], two_steps, 0)
    wait_all(incoming[2:])

    wide = lane_iota((lanes, across))
    border = (wide == 0) | (wide == across - 1)

    def place(x):
        return [
            pltpu.make_async_copy(field.at[c, x], deposit_hbm.at[c, x], sems.at[c, x])
            for c in range(components)
        ]

    def combine(x, carry):
        for c in range(components):
            for p in range(parts):
                part = slice(p * lanes, (p + 1) * lanes)
                high = total[x, c * across : (c + 1) * across, part]
                low = total[x, (components + c) * across : (components + c + 1) * across, part]
                value = (high + low).T
                field[c, x, part, :] = value.astype(jnp.bfloat16)
                edge = pltpu.roll(edges[part, :], lanes - 1 - 2 * (c * planes + x), 1)
                rhs[c, x, part, :] = rhs[c, x, part, :] + value + jnp.where(border, edge, 0.0)
        start_all(place(x))
        return carry

    lax.fori_loop(0, planes, combine, 0)
    sums[2 * lines : 2 * lines + coefs.shape[0], :] = coefs[...]

    zero = jnp.zeros((components, planes, segments, across), jnp.float32)

    def of_step(t):
        return rhs[:, :, pl.ds(t, segments, stride=steps), :]

    def forward(t, carry):
        value, start, run, before = carry
        force = of_step(t)
        low, inverse = lower[:, pl.ds(t, segments, stride=steps), :], inv[t]
        value = force + (low * before)[None] * value
        swept[t] = inverse[None] * value
        run = run * (low * inverse)
        prefix[t] = run
        return value, start + first[t][None] * force, run, inverse

    one = jnp.ones((planes, segments, across), jnp.float32)
    value, start, _, inverse = lax.fori_loop(0, last, forward, (zero, zero, one, one), unroll=3)
    value = inverse[None] * value
    segment = lax.broadcasted_iota(jnp.int32, zero.shape, 2)
    after = jnp.where(segment == segments - 1, 0.0, jnp.roll(start, -1, axis=2))
    low_sep, up_sep = ends[2, :, :segments, :], ends[3, :, :segments, :]
    value = of_step(last) + low_sep[None] * value + up_sep[None] * after
    others = rhs[:, :, height - rest :, :]
    at_top = ends[0, :, :segments, :][None] * value + ends[0, :, segments:, :][None] * others
    at_bottom = ends[1, :, :segments, :][None] * value + ends[1, :, segments:, :][None] * others
    at_bottom = at_bottom + jnp.where(segment == 0, start, 0.0)
    for c in range(components):
        for x in range(planes):
            k = c * planes + x
            reduced[k * knots : k * knots + segments, :] = value[c, x]
            reduced[k * knots + segments : (k + 1) * knots, :] = others[c, x]
            sums[k : k + 1, :] = jnp.sum(at_top[c, x], 0, keepdims=True)
            sums[lines + k : lines + k + 1, :] = jnp.sum(at_bottom[c, x], 0, keepdims=True)

    for x in range(planes):
        wait_all(place(x))


def finish_kernel(inner, reduced, swept, inv, prefix, upper, *refs):
    walls = len(refs) - 7
    received = refs[:walls]
    out_hbm, sums, tops, after, before, out, sems = refs[walls:]
    components, planes, height, across = out.shape
    steps = swept.shape[0] + 1
    last = steps - 1
    lines = components * planes
    knots = inner.shape[1] + 1
    rest = knots - segments
    me = lax.axis_index("wall")
    for n in range(walls):
        sums[lax.rem(me + walls - n, walls)] = received[n][...]

    def coef(k, n):
        start = 2 * lines + n * planes
        return sums[k, start : start + planes, :]

    def wide(value):
        return jnp.concatenate([value] * components, 0)

    d = jnp.ones((planes, across), jnp.float32)
    value = jnp.zeros((lines, across), jnp.float32)
    values, ratios = [], []
    for k in range(walls):
        low, own, up = coef(k, 0), coef(k, 1), coef(k, 2)
        right = sums[k, :lines, :]
        if k + 1 < walls:
            high = up * coef(k + 1, 4)
            killing = own + up * coef(k + 1, 3)
            right = right + wide(up) * sums[k + 1, lines : 2 * lines, :]
        else:
            high = jnp.zeros_like(up)
            killing = own + up
        e = killing + low * d
        inverse = reciprocal(high + e)
        d = e * inverse
        value = (right + wide(low) * value) * wide(inverse)
        values.append(value)
        ratios.append(wide(high * inverse))
    tops[0] = jnp.zeros((lines, across), jnp.float32)
    tops[walls] = values[-1]
    for k in reversed(range(walls - 1)):
        values[k] = values[k] + ratios[k] * values[k + 1]
        tops[k + 1] = values[k]

    def row(s):
        return pl.ds(s, lines, stride=knots)

    run = tops[me]
    before[row(0), :] = run
    found = []
    for s in range(knots - 1):
        run = reduced[row(s), :] * wide(inner[0, s]) + wide(inner[1, s]) * run
        found.append(run)
    run = tops[me + 1]
    after[row(knots - 1), :] = run
    for s in reversed(range(knots - 1)):
        run = found[s] + wide(inner[2, s]) * run
        after[row(s), :] = run
        if s + 1 < segments:
            before[row(s + 1), :] = run

    def put(c, x, t, value):
        out[c, x, pl.ds(t, segments, stride=steps), :] = value

    copies = []
    half = planes // 2 if planes % 2 == 0 else planes
    for start in range(0, planes, half):
        part = [(c, x) for c in range(components) for x in range(start, start + half)]
        bottoms, starts = [], []
        for c, x in part:
            base = (c * planes + x) * knots
            bottoms.append(before[base : base + segments, :])
            starts.append(after[base : base + segments, :])
            out[c, x, height - rest :, :] = after[base + segments : base + knots, :]
            put(c, x, last, starts[-1])

        def backward(n, values):
            t = last - 1 - n
            found = []
            ratios = {}
            for x in range(start, start + half):
                ratios[x] = upper[x, pl.ds(t, segments, stride=steps), :] * inv[t, x]
            for (c, x), value, bottom in zip(part, values, bottoms):
                value = (swept[t, c, x] + prefix[t, x] * bottom) + ratios[x] * value
                put(c, x, t, value)
                found.append(value)
            return tuple(found)

        lax.fori_loop(0, last, backward, tuple(starts), unroll=3)
        for here in part:
            copy = pltpu.make_async_copy(out.at[here], out_hbm.at[here], sems.at[here])
            copy.start()
            copies.append(copy)
    wait_all(copies)


def everyone(block, axis, by_distance):
    length = lax.axis_size(axis)
    found = [by_distance[0]]
    for distance in range(1, length):
        route = [(i, (i + distance) % length) for i in range(length)]
        found.append(lax.ppermute(by_distance[distance], axis, route))
    return found


def local(velocity, lower_weight, upper_weight, forces, cells, counts):
    components, planes, height, across = velocity.shape
    receivers, capacity = forces.shape[3], forces.shape[5]
    senders = cells.shape[2]
    walls = lax.axis_size("wall")
    lines = components * planes
    chunks = capacity // lanes
    slot = components + 1
    forces = forces.reshape(components, receivers, planes, capacity)
    cells = cells.reshape(senders, planes, capacity)
    counts = counts.reshape(senders, planes).T

    def hbm(*arrays):
        return [pltpu.with_memory_space_constraint(array, pltpu.HBM) for array in arrays]

    send, velocity_near = call(
        pack_kernel,
        (f32(receivers, planes * chunks * slot, lanes), f32(*velocity.shape)),
        (in_hbm, in_vmem),
        [in_hbm] * 2,
        [
            scratch(*forces.shape),
            scratch(receivers, planes * chunks * slot, lanes),
            scratch(height, across),
            scratch(height // lanes, lanes, lanes),
            pltpu.SemaphoreType.DMA((components + lines + receivers,)),
        ],
        8,
        1 << 22,
    )(*hbm(velocity, forces))
    got = lax.all_to_all(send, "span", 0, 0, tiled=True)

    steps = height // segments - 1
    knots = height - segments * steps + segments
    step_shape = (steps - 1, planes, segments, across)
    work_shape = (planes * (senders * chunks + group) + 4 * group,)
    staged = [
        (velocity.shape, jnp.float32),
        (step_shape, jnp.float32),
        (step_shape, jnp.float32),
        ((3, knots - 1, planes, across), jnp.float32),
        ((4, planes, knots, across), jnp.float32),
        ((5 * planes, across), jnp.float32),
        ((senders * planes * chunks, lanes), jnp.int32),
    ]
    prepared = call(
        prepare_kernel,
        [pltpu.HBM(*entry) for entry in staged] + [pltpu.HBM(work_shape, jnp.int32)],
        [in_hbm] * 8,
        [in_smem, in_hbm] + [in_vmem] * 3,
        [
            *[pltpu.VMEM(*entry) for entry in staged],
            pltpu.SMEM(work_shape, jnp.int32),
            pltpu.VMEM(cells.shape, jnp.int32),
            scratch(*step_shape),
            scratch(*step_shape),
            scratch(7, planes * knots, across),
            pltpu.SemaphoreType.DMA((9,)),
        ],
        12,
        1 << 24,
    )(counts, *hbm(cells), velocity_near, lower_weight, upper_weight)
    (rhs_start, inv, first, inner, ends, coefs, cell_rows, work) = prepared

    sum_rows = -(-(2 * lines + 5 * planes) // 8) * 8
    wide = 2 * components * across
    deposit, swept, prefix, reduced, sums = call(
        deposit_kernel,
        (
            jax.ShapeDtypeStruct(velocity.shape, jnp.bfloat16),
            f32(steps - 1, components, planes, segments, across),
            f32(*step_shape),
            f32(lines * knots, across),
            f32(sum_rows, across),
        ),
        (in_hbm, *[in_vmem] * 4),
        [in_vmem] + [in_hbm] * 8,
        [
            pltpu.SMEM(work_shape, jnp.int32),
            pltpu.VMEM(*staged[6]),
            *[pltpu.VMEM(*staged[n]) for n in (0, 1, 2, 4, 5)],
            scratch(*lower_weight.shape),
            pltpu.VMEM(velocity.shape, jnp.bfloat16),
            scratch(planes, wide, height),
            [pltpu.VMEM((height, group * lanes), jnp.bfloat16)] * 2,
            [pltpu.VMEM((wide, group * lanes), jnp.bfloat16)] * 2,
            scratch(height // lanes, lanes, lanes),
            scratch(height, lanes),
            pltpu.SemaphoreType.DMA((8,)),
            pltpu.SemaphoreType.DMA((components, planes)),
        ],
        24,
        1 << 32,
    )(
        got.reshape(-1, lanes),
        *hbm(work, cell_rows, rhs_start, inv, first, ends, coefs, lower_weight),
    )
    all_sums = everyone(sums, "wall", [sums] * walls)

    velocity_next = call(
        finish_kernel,
        f32(*velocity.shape),
        in_hbm,
        [in_vmem] * (6 + walls),
        [
            scratch(walls, sum_rows, across),
            scratch(walls + 1, lines, across),
            scratch(lines * knots, across),
            scratch(lines * knots, across),
            scratch(*velocity.shape),
            pltpu.SemaphoreType.DMA((components, planes)),
        ],
        8,
        1 << 22,
    )(inner, reduced, swept, inv, prefix, upper_weight, *all_sums)
    return (velocity_next, deposit)


def solution(mesh):
    placed = (
        P(None, None, "wall", "span"),
        P(None, "wall", "span"),
        P(None, "wall", "span"),
        P(None, "wall", "span", None, None, None),
        P("wall", "span", None, None, None),
        P("wall", "span", None, None),
    )
    return jax.shard_map(
        local,
        mesh=mesh,
        in_specs=placed,
        out_specs=(P(None, None, "wall", "span"), P(None, None, "wall", "span")),
        check_vma=False,
    )
```

profile of v0, /device:TPU:0, one launch (start us, length us, event | category | flops | bytes accessed | tf_op | source)
XLA Modules:
  0.0 42.5 jit_solution(13209919772839214401)
XLA Ops:
  0.6 0.0 copy-start
  0.6 0.0 copy-start.1
  0.7 0.0 copy-start.4
  0.7 3.2 %shard_map.77 = (f32[8,96,128]{2,1,0:T(8,128)}, f32[3,4,256,128]{3,2,1,0:T(8,128)S(1)}) custom-call(f32[3,4,256,128]{3,2,1,0:T(8,128)} %velocity_hbm.1, f32[3,8,4,768]{3,2,1,0:T(4,128)} %bitcast.8), custom_call_target="tpu_custom_call" | custom-call | flops 4194304 | bytes 4194304 | tf_op jit(solution)/shard_map/pallas_call | solution.py:573
  3.9 5.2 %all-to-all-start = ((f32[8,96,128]{2,1,0:T(8,128)}), f32[8,96,128]{2,1,0:T(8,128)S(1)}, u32[]{:S(2)}, u32[]{:S(2)}) async-start(f32[8,96,128]{2,1,0:T(8,128)} %get-tuple-element.19), calls=%async_computation | async-start | bytes 786432 | tf_op jit(solution)/shard_map/all_to_all | solution.py:588
  9.1 0.0 copy-done
  9.1 0.0 copy-done.1
  9.1 0.0 copy-done.4
  9.1 6.0 %shard_map.78 = (f32[3,4,256,128]{3,2,1,0:T(8,128)}, f32[30,4,8,128]{3,2,1,0:T(8,128)}, f32[30,4,8,128]{3,2,1,0:T(8,128)}, f32[3,15,4,128]{3,2,1,0:T(4,128)}, f3...) custom-call(s32[4,8]{1,0:T(4,128)S(1)} %bitcast.7, s32[8,4,768]{2,1,0:T(4,128)} %bitcast.9, ...), custom_call_target="tpu_custom_call" | custom-call | flops 16777216 | bytes 4194304 | tf_op jit(solution)/shard_map/pallas_call | solution.py:603
  15.1 2.3 %all-to-all-done = f32[8,96,128]{2,1,0:T(8,128)S(1)} async-done(((f32[8,96,128]{2,1,0:T(8,128)}), f32[8,96,128]{2,1,0:T(8,128)S(1)}, u32[]{:S(2)}, u32[]{:S(2)}) %all-to-all-start) | async-done | bytes 393248 | tf_op jit(solution)/shard_map/all_to_all | solution.py:588
  17.4 0.0 copy-start.2
  17.4 0.0 copy-start.3
  17.4 8.3 %shard_map.79 = (bf16[3,4,256,128]{3,2,1,0:T(8,128)(2,1)}, f32[30,3,4,8,128]{4,3,2,1,0:T(8,128)S(1)}, f32[30,4,8,128]{3,2,1,0:T(8,128)S(1)}, f32[192,128]{1,0:T(8,128)S(1)}, f32[48,128]{1,0:T(8,128)S(1)}) custom-call(f32[768,128]{1,0:T(8,128)S(1)} %bitcast.6, s32[224]{0:T(256)} %get-tuple-element.20.refs_0_, s32[192,128]{1,0:T(8,128)} %get-tuple-element.21.refs_1_, ...), custom_call_target="tpu_custom_call" | custom-call | flops 4294967296 | bytes 4194304 | tf_op jit(solution)/shard_map/pallas_call | solution.py:624
  25.7 9.5 %collective-permute-start.2 = (f32[48,128]{1,0:T(8,128)S(1)}, f32[48,128]{1,0:T(8,128)S(1)}, u32[]{:S(2)}, u32[]{:S(2)}) collective-permute-start(f32[48,128]{1,0:T(8,128)S(1)} %get-tuple-element.30.refs_0_), channel_id=1, source_target_pairs={{0,24},{8,0},{16,8},{24,16},{1,25},{9,1},{17,9},{25,17},{2,26},{10... | collective-permute-start | bytes 73736 | tf_op jit(solution)/shard_map/ppermute | solution.py:554
  35.3 0.0 collective-permute-start.1
  35.3 0.6 %collective-permute-start = (f32[48,128]{1,0:T(8,128)S(1)}, f32[48,128]{1,0:T(8,128)S(1)}, u32[]{:S(2)}, u32[]{:S(2)}) collective-permute-start(f32[48,128]{1,0:T(8,128)S(1)} %get-tuple-element.30.refs_0_), channel_id=1, source_target_pairs={{0,8},{8,16},{16,24},{24,0},{1,9},{9,17},{17,25},{25,1},{2,10},{10... | collective-permute-start | bytes 73736 | tf_op jit(solution)/shard_map/ppermute | solution.py:554
  35.9 0.9 %collective-permute-done.2.refs_3_ = f32[48,128]{1,0:T(8,128)S(1)} collective-permute-done((f32[48,128]{1,0:T(8,128)S(1)}, f32[48,128]{1,0:T(8,128)S(1)}, u32[]{:S(2)}, u32[]{:S(2)}) %collective-permute-start.2) | collective-permute-done | bytes 24608 | tf_op jit(solution)/shard_map/ppermute | solution.py:554
  36.8 3.2 %collective-permute-done.1.refs_2_ = f32[48,128]{1,0:T(8,128)S(1)} collective-permute-done((f32[48,128]{1,0:T(8,128)S(1)}, f32[48,128]{1,0:T(8,128)S(1)}, u32[]{:S(2)}, u32[]{:S(2)}) %collective-permute-start.1) | collective-permute-done | bytes 24608 | tf_op jit(solution)/shard_map/ppermute | solution.py:554
  40.0 0.9 %collective-permute-done.refs_1_ = f32[48,128]{1,0:T(8,128)S(1)} collective-permute-done((f32[48,128]{1,0:T(8,128)S(1)}, f32[48,128]{1,0:T(8,128)S(1)}, u32[]{:S(2)}, u32[]{:S(2)}) %collective-permute-start) | collective-permute-done | bytes 24608 | tf_op jit(solution)/shard_map/ppermute | solution.py:554
  40.9 0.0 copy-done.2
  40.9 0.0 copy-done.3
  40.9 1.6 %shard_map.80 = f32[3,4,256,128]{3,2,1,0:T(8,128)} custom-call(f32[3,15,4,128]{3,2,1,0:T(4,128)S(1)} %copy-done.3, f32[192,128]{1,0:T(8,128)S(1)} %get-tuple-element.27.reduced, f32[30,3,4,8,128]{4,3,2,1,0:T(8,128)S(1)} %get-tuple-element.28.swept, f32[30,4,8,128]{3,2,1,0:T(8,128)S(1)} %copy-done.2, f32[30,4,8,128]{3,2,1,0:T(8,128)S(1)} %get-tuple-element.29.prefix, ...), custom_call_target="tpu_custom_call" | custom-call | flops 4194304 | bytes 4194304 | tf_op jit(solution)/shard_map/pallas_call | solution.py:657
Async XLA Ops:
  0.6 8.5 %copy-start = (f32[4,256,128]{2,1,0:T(8,128)S(1)}, f32[4,256,128]{2,1,0:T(8,128)}, u32[]{:S(2)}) copy-start(f32[4,256,128]{2,1,0:T(8,128)} %upper.3) | copy-start | bytes 1572868
  0.6 8.5 %copy-start.1 = (f32[4,256,128]{2,1,0:T(8,128)S(1)}, f32[4,256,128]{2,1,0:T(8,128)}, u32[]{:S(2)}) copy-start(f32[4,256,128]{2,1,0:T(8,128)} %refs_7_.1) | copy-start | bytes 1572868
  0.7 8.5 %copy-start.4 = (s32[1,1,8,4]{2,3,1,0:T(4,128)S(1)}, s32[1,1,8,4]{2,3,1,0:T(4,128)}, u32[]{:S(2)}) copy-start(s32[1,1,8,4]{2,3,1,0:T(4,128)} %param.11) | copy-start | bytes 388
  3.9 13.5 %all-to-all-start = ((f32[8,96,128]{2,1,0:T(8,128)}), f32[8,96,128]{2,1,0:T(8,128)S(1)}, u32[]{:S(2)}, u32[]{:S(2)}) async-start(f32[8,96,128]{2,1,0:T(8,128)} %get-tuple-element.19), calls=%async_computation | async-start | bytes 786432 | tf_op jit(solution)/shard_map/all_to_all | solution.py:588
  17.4 23.4 %copy-start.2 = (f32[30,4,8,128]{3,2,1,0:T(8,128)S(1)}, f32[30,4,8,128]{3,2,1,0:T(8,128)}, u32[]{:S(2)}) copy-start(f32[30,4,8,128]{3,2,1,0:T(8,128)} %get-tuple-element.23.refs_3_.inv) | copy-start | bytes 1474564
  17.4 23.4 %copy-start.3 = (f32[3,15,4,128]{3,2,1,0:T(4,128)S(1)}, f32[3,15,4,128]{3,2,1,0:T(4,128)}, u32[]{:S(2)}) copy-start(f32[3,15,4,128]{3,2,1,0:T(4,128)} %get-tuple-element.18.inner) | copy-start | bytes 276484
  25.7 11.1 %collective-permute-start.2 = (f32[48,128]{1,0:T(8,128)S(1)}, f32[48,128]{1,0:T(8,128)S(1)}, u32[]{:S(2)}, u32[]{:S(2)}) collective-permute-start(f32[48,128]{1,0:T(8,128)S(1)} %get-tuple-element.30.refs_0_), channel_id=1, source_target_pairs={{0,24},{8,0},{16,8},{24,16},{1,25},{9,1},{17,9},{25,17},{2,26},{10... | collective-permute-start | bytes 73736 | tf_op jit(solution)/shard_map/ppermute | solution.py:554
  35.3 4.7 %collective-permute-start.1 = (f32[48,128]{1,0:T(8,128)S(1)}, f32[48,128]{1,0:T(8,128)S(1)}, u32[]{:S(2)}, u32[]{:S(2)}) collective-permute-start(f32[48,128]{1,0:T(8,128)S(1)} %get-tuple-element.30.refs_0_), channel_id=1, source_target_pairs={{0,16},{8,24},{16,0},{24,8},{1,17},{9,25},{17,1},{25,9},{2,18},{10... | collective-permute-start | bytes 73736 | tf_op jit(solution)/shard_map/ppermute | solution.py:554
  35.3 5.6 %collective-permute-start = (f32[48,128]{1,0:T(8,128)S(1)}, f32[48,128]{1,0:T(8,128)S(1)}, u32[]{:S(2)}, u32[]{:S(2)}) collective-permute-start(f32[48,128]{1,0:T(8,128)S(1)} %get-tuple-element.30.refs_0_), channel_id=1, source_target_pairs={{0,8},{8,16},{16,24},{24,0},{1,9},{9,17},{17,25},{25,1},{2,10},{10... | collective-permute-start | bytes 73736 | tf_op jit(solution)/shard_map/ppermute | solution.py:554
where the time goes:
time: 42.4 us; the launch traced here: 42.5 us
  Pallas kernels  19.1 us (45%)
  starting transfers between devices  15.4 us (36%)
  waiting for transfers between devices  7.28 us (17%)
  between operations  0.7 us (2%)
    ppermute x3, starting transfers between devices, everyone(): found.append(lax.ppermute(by_distance[distance], axis, route))  10.2 us
    pallas_call x1, Pallas kernels, local(): call(deposit_kernel, (jax.ShapeDtypeStruct(velocity.shape, jnp.bfloat16),...  8.26 us
    pallas_call x1, Pallas kernels, local(): call(prepare_kernel, [pltpu.HBM(*entry) for entry in staged] + [pltpu.HBM...  6.01 us
    all_to_all x1, starting transfers between devices, local(): got = lax.all_to_all(send, 'span', 0, 0, tiled=True)  5.18 us
    ppermute x3, waiting for transfers between devices, everyone(): found.append(lax.ppermute(by_distance[distance], axis, route))  4.98 us
    pallas_call x1, Pallas kernels, local(): call(pack_kernel, (f32(receivers, planes * chunks * slot, lanes), f32(*ve...  3.25 us
    all_to_all x1, waiting for transfers between devices, local(): got = lax.all_to_all(send, 'span', 0, 0, tiled=True)  2.3 us
    pallas_call x1, Pallas kernels, local(): call(finish_kernel, f32(*velocity.shape), in_hbm, [in_vmem] * (6 + walls)...  1.58 us
  transfers between devices with their start and end apart: 4, of which 4 were waited for; matrix products, arithmetic and copies ran while one was open for 0% of the time, Pallas kernels for 14%

commit v1 on v0

--- a/solution.py
+++ b/solution.py
@@ -305,7 +305,7 @@
 def deposit_kernel(got, *refs):
     (deposit_hbm, swept, prefix, reduced, sums) = refs[8:13]
     (work, cell_rows, rhs, inv, first, ends, coefs, lower) = refs[13:21]
-    (field, total, lefts, rights, columns, edges, in_sems, sems) = refs[21:]
+    (field, total, ups, lefts, rights, columns, edges, in_sems, sems) = refs[21:]
     incoming = copies_of(refs[:8], refs[13:21], in_sems)
     start_all(incoming)
     components, planes, height, across = rhs.shape
@@ -319,12 +319,14 @@
     parts = height // lanes
     shift = across.bit_length() - 1
     lines = components * planes
-    kind = jnp.bfloat16 if max(height, across) <= 256 else jnp.float32
+    kind = jnp.bfloat16 if across <= 256 else jnp.float32
 
     me = lax.axis_index("span")
     below = lax.rem(me + senders - 1, senders)
     above = lax.rem(me + 1, senders)
     total[...] = jnp.zeros_like(total)
+    for half in range(2):
+        ups[half][...] = jnp.zeros((8, lanes), jnp.float32)
     for p in range(parts):
         for n, owner in enumerate((above, below)):
             start = owner * block + p * slot + components
@@ -333,10 +335,9 @@
 
     tile = 16
     base = lax.broadcasted_iota(jnp.int32, (tile, lanes), 0)
-    height_ids = [(base + n * tile).astype(jnp.float32).astype(kind) for n in range(height // tile)]
-    across_ids = height_ids[: across // tile]
+    across_ids = [(base + n * tile).astype(jnp.float32).astype(kind) for n in range(across // tile)]
+    every_height = lane_iota((lanes, height)).astype(jnp.float32)
     lane = lane_iota((1, lanes))
-    one = jnp.ones((tile, lanes), jnp.bfloat16)
     none = jnp.zeros((tile, lanes), jnp.bfloat16)
 
     def spread(row, to):
@@ -351,9 +352,8 @@
             cell = cell_rows[pl.ds(ident, 1), :]
             up = jnp.where(lane < live, cell >> shift, -1).astype(jnp.float32)
             side = (cell & (across - 1)).astype(jnp.float32)
-            up, side = spread(up, kind), spread(side, kind)
-            for i, ids in enumerate(height_ids):
-                lefts[half][i * tile : (i + 1) * tile, there] = jnp.where(up == ids, one, none)
+            ups[half][g : g + 1, :] = up
+            side = spread(side, kind)
             masks = [side == ids for ids in across_ids]
             for c in range(components):
                 force = got[pl.ds(ident * slot + c, 1), :]
@@ -364,12 +364,16 @@
                     for i, mask in enumerate(masks):
                         place = slice(start + i * tile, start + (i + 1) * tile)
                         rights[half][place, there] = jnp.where(mask, value, none)
+        turned = ups[half][...].T
+        for g in range(group):
+            hot = jnp.where(turned[:, g : g + 1] == every_height, 1.0, 0.0)
+            lefts[half][g * lanes : (g + 1) * lanes, :] = hot.astype(jnp.bfloat16)
 
     def add(n, half):
         total[work[(n + 1) * group] >> plane_bit] += lax.dot_general(
             rights[half][...],
             lefts[half][...],
-            (((1,), (1,)), ((), ())),
+            (((1,), (0,)), ((), ())),
             preferred_element_type=jnp.float32,
         )
 
@@ -639,7 +643,8 @@
             scratch(*lower_weight.shape),
             pltpu.VMEM(velocity.shape, jnp.bfloat16),
             scratch(planes, wide, height),
-            [pltpu.VMEM((height, group * lanes), jnp.bfloat16)] * 2,
+            [scratch(8, lanes)] * 2,
+            [pltpu.VMEM((group * lanes, height), jnp.bfloat16)] * 2,
             [pltpu.VMEM((wide, group * lanes), jnp.bfloat16)] * 2,
             scratch(height // lanes, lanes, lanes),
             scratch(height, lanes),

time: 42.4 us -> 44.5 us (1.050); the launches traced: 42.5 us -> 45.3 us
  starting transfers between devices: 15.4 us -> 17.2 us
  Pallas kernels: 19.1 us -> 20.1 us
    ppermute x3, starting transfers between devices: 10.2 us -> 12 us  [everyone(): found.append(lax.ppermute(by_distance[distance], axis, route))]
    pallas_call x1, Pallas kernels: 8.26 us -> 9.27 us  [local(): call(deposit_kernel, (jax.ShapeDtypeStruct(velocity.shape, jnp.bfloat16),...]
  transfers between devices with their start and end apart: 4 -> 4, of which waited for: 4 -> 4; matrix products, arithmetic and copies ran while one was open for 0% -> 0% of each run, Pallas kernels for 14% -> 13%
where the time goes in v1:
time: 44.5 us; the launch traced here: 45.3 us
  Pallas kernels  20.1 us (45%)
  starting transfers between devices  17.2 us (39%)
  waiting for transfers between devices  7.28 us (16%)
  between operations  0.7 us (2%)
    ppermute x3, starting transfers between devices, everyone(): found.append(lax.ppermute(by_distance[distance], axis, route))  12 us
    pallas_call x1, Pallas kernels, local(): call(deposit_kernel, (jax.ShapeDtypeStruct(velocity.shape, jnp.bfloat16),...  9.27 us
    pallas_call x1, Pallas kernels, local(): call(prepare_kernel, [pltpu.HBM(*entry) for entry in staged] + [pltpu.HBM...  6.01 us
    all_to_all x1, starting transfers between devices, local(): got = lax.all_to_all(send, 'span', 0, 0, tiled=True)  5.18 us
    ppermute x3, waiting for transfers between devices, everyone(): found.append(lax.ppermute(by_distance[distance], axis, route))  4.98 us
    pallas_call x1, Pallas kernels, local(): call(pack_kernel, (f32(receivers, planes * chunks * slot, lanes), f32(*ve...  3.25 us
    all_to_all x1, waiting for transfers between devices, local(): got = lax.all_to_all(send, 'span', 0, 0, tiled=True)  2.3 us
    pallas_call x1, Pallas kernels, local(): call(finish_kernel, f32(*velocity.shape), in_hbm, [in_vmem] * (6 + walls)...  1.58 us
  transfers between devices with their start and end apart: 4, of which 4 were waited for; matrix products, arithmetic and copies ran while one was open for 0% of the time, Pallas kernels for 13%

profile of v1, /device:TPU:0, one launch (start us, length us, event | category | flops | bytes accessed | tf_op | source)
XLA Modules:
  0.0 45.3 jit_solution(11875797320635724612)
XLA Ops:
  0.6 0.0 copy-start
  0.6 0.0 copy-start.1
  0.7 0.0 copy-start.4
  0.7 3.2 %shard_map.77 = (f32[8,96,128]{2,1,0:T(8,128)}, f32[3,4,256,128]{3,2,1,0:T(8,128)S(1)}) custom-call(f32[3,4,256,128]{3,2,1,0:T(8,128)} %velocity_hbm.1, f32[3,8,4,768]{3,2,1,0:T(4,128)} %bitcast.8), custom_call_target="tpu_custom_call" | custom-call | flops 4194304 | bytes 4194304 | tf_op jit(solution)/shard_map/pallas_call | solution.py:577
  3.9 5.2 %all-to-all-start = ((f32[8,96,128]{2,1,0:T(8,128)}), f32[8,96,128]{2,1,0:T(8,128)S(1)}, u32[]{:S(2)}, u32[]{:S(2)}) async-start(f32[8,96,128]{2,1,0:T(8,128)} %get-tuple-element.19), calls=%async_computation | async-start | bytes 786432 | tf_op jit(solution)/shard_map/all_to_all | solution.py:592
  9.1 0.0 copy-done
  9.1 0.0 copy-done.1
  9.1 0.0 copy-done.4
  9.1 6.0 %shard_map.78 = (f32[3,4,256,128]{3,2,1,0:T(8,128)}, f32[30,4,8,128]{3,2,1,0:T(8,128)}, f32[30,4,8,128]{3,2,1,0:T(8,128)}, f32[3,15,4,128]{3,2,1,0:T(4,128)}, f3...) custom-call(s32[4,8]{1,0:T(4,128)S(1)} %bitcast.7, s32[8,4,768]{2,1,0:T(4,128)} %bitcast.9, ...), custom_call_target="tpu_custom_call" | custom-call | flops 16777216 | bytes 4194304 | tf_op jit(solution)/shard_map/pallas_call | solution.py:607
  15.1 2.3 %all-to-all-done = f32[8,96,128]{2,1,0:T(8,128)S(1)} async-done(((f32[8,96,128]{2,1,0:T(8,128)}), f32[8,96,128]{2,1,0:T(8,128)S(1)}, u32[]{:S(2)}, u32[]{:S(2)}) %all-to-all-start) | async-done | bytes 393248 | tf_op jit(solution)/shard_map/all_to_all | solution.py:592
  17.4 0.0 copy-start.2
  17.4 0.0 copy-start.3
  17.4 9.3 %shard_map.79 = (bf16[3,4,256,128]{3,2,1,0:T(8,128)(2,1)}, f32[30,3,4,8,128]{4,3,2,1,0:T(8,128)S(1)}, f32[30,4,8,128]{3,2,1,0:T(8,128)S(1)}, f32[192,128]{1,0:T(8,128)S(1)}, f32[48,128]{1,0:T(8,128)S(1)}) custom-call(f32[768,128]{1,0:T(8,128)S(1)} %bitcast.6, s32[224]{0:T(256)} %get-tuple-element.20.refs_0_, s32[192,128]{1,0:T(8,128)} %get-tuple-element.21.refs_1_, ...), custom_call_target="tpu_custom_call" | custom-call | flops 4294967296 | bytes 4194304 | tf_op jit(solution)/shard_map/pallas_call | solution.py:628
  26.7 11.3 %collective-permute-start.2 = (f32[48,128]{1,0:T(8,128)S(1)}, f32[48,128]{1,0:T(8,128)S(1)}, u32[]{:S(2)}, u32[]{:S(2)}) collective-permute-start(f32[48,128]{1,0:T(8,128)S(1)} %get-tuple-element.30.refs_0_), channel_id=1, source_target_pairs={{0,24},{8,0},{16,8},{24,16},{1,25},{9,1},{17,9},{25,17},{2,26},{10... | collective-permute-start | bytes 73736 | tf_op jit(solution)/shard_map/ppermute | solution.py:558
  38.1 0.0 collective-permute-start.1
  38.1 0.6 %collective-permute-start = (f32[48,128]{1,0:T(8,128)S(1)}, f32[48,128]{1,0:T(8,128)S(1)}, u32[]{:S(2)}, u32[]{:S(2)}) collective-permute-start(f32[48,128]{1,0:T(8,128)S(1)} %get-tuple-element.30.refs_0_), channel_id=1, source_target_pairs={{0,8},{8,16},{16,24},{24,0},{1,9},{9,17},{17,25},{25,1},{2,10},{10... | collective-permute-start | bytes 73736 | tf_op jit(solution)/shard_map/ppermute | solution.py:558
  38.7 0.9 %collective-permute-done.2.refs_3_ = f32[48,128]{1,0:T(8,128)S(1)} collective-permute-done((f32[48,128]{1,0:T(8,128)S(1)}, f32[48,128]{1,0:T(8,128)S(1)}, u32[]{:S(2)}, u32[]{:S(2)}) %collective-permute-start.2) | collective-permute-done | bytes 24608 | tf_op jit(solution)/shard_map/ppermute | solution.py:558
  39.6 3.2 %collective-permute-done.1.refs_2_ = f32[48,128]{1,0:T(8,128)S(1)} collective-permute-done((f32[48,128]{1,0:T(8,128)S(1)}, f32[48,128]{1,0:T(8,128)S(1)}, u32[]{:S(2)}, u32[]{:S(2)}) %collective-permute-start.1) | collective-permute-done | bytes 24608 | tf_op jit(solution)/shard_map/ppermute | solution.py:558
  42.8 0.9 %collective-permute-done.refs_1_ = f32[48,128]{1,0:T(8,128)S(1)} collective-permute-done((f32[48,128]{1,0:T(8,128)S(1)}, f32[48,128]{1,0:T(8,128)S(1)}, u32[]{:S(2)}, u32[]{:S(2)}) %collective-permute-start) | collective-permute-done | bytes 24608 | tf_op jit(solution)/shard_map/ppermute | solution.py:558
  43.7 0.0 copy-done.2
  43.7 0.0 copy-done.3
  43.7 1.6 %shard_map.80 = f32[3,4,256,128]{3,2,1,0:T(8,128)} custom-call(f32[3,15,4,128]{3,2,1,0:T(4,128)S(1)} %copy-done.3, f32[192,128]{1,0:T(8,128)S(1)} %get-tuple-element.27.reduced, f32[30,3,4,8,128]{4,3,2,1,0:T(8,128)S(1)} %get-tuple-element.28.swept, f32[30,4,8,128]{3,2,1,0:T(8,128)S(1)} %copy-done.2, f32[30,4,8,128]{3,2,1,0:T(8,128)S(1)} %get-tuple-element.29.prefix, ...), custom_call_target="tpu_custom_call" | custom-call | flops 4194304 | bytes 4194304 | tf_op jit(solution)/shard_map/pallas_call | solution.py:662
Async XLA Ops:
  0.6 8.5 %copy-start = (f32[4,256,128]{2,1,0:T(8,128)S(1)}, f32[4,256,128]{2,1,0:T(8,128)}, u32[]{:S(2)}) copy-start(f32[4,256,128]{2,1,0:T(8,128)} %upper.3) | copy-start | bytes 1572868
  0.6 8.5 %copy-start.1 = (f32[4,256,128]{2,1,0:T(8,128)S(1)}, f32[4,256,128]{2,1,0:T(8,128)}, u32[]{:S(2)}) copy-start(f32[4,256,128]{2,1,0:T(8,128)} %refs_7_.1) | copy-start | bytes 1572868
  0.7 8.5 %copy-start.4 = (s32[1,1,8,4]{2,3,1,0:T(4,128)S(1)}, s32[1,1,8,4]{2,3,1,0:T(4,128)}, u32[]{:S(2)}) copy-start(s32[1,1,8,4]{2,3,1,0:T(4,128)} %param.11) | copy-start | bytes 388
  3.9 13.5 %all-to-all-start = ((f32[8,96,128]{2,1,0:T(8,128)}), f32[8,96,128]{2,1,0:T(8,128)S(1)}, u32[]{:S(2)}, u32[]{:S(2)}) async-start(f32[8,96,128]{2,1,0:T(8,128)} %get-tuple-element.19), calls=%async_computation | async-start | bytes 786432 | tf_op jit(solution)/shard_map/all_to_all | solution.py:592
  17.4 26.2 %copy-start.2 = (f32[30,4,8,128]{3,2,1,0:T(8,128)S(1)}, f32[30,4,8,128]{3,2,1,0:T(8,128)}, u32[]{:S(2)}) copy-start(f32[30,4,8,128]{3,2,1,0:T(8,128)} %get-tuple-element.23.refs_3_.inv) | copy-start | bytes 1474564
  17.4 26.2 %copy-start.3 = (f32[3,15,4,128]{3,2,1,0:T(4,128)S(1)}, f32[3,15,4,128]{3,2,1,0:T(4,128)}, u32[]{:S(2)}) copy-start(f32[3,15,4,128]{3,2,1,0:T(4,128)} %get-tuple-element.18.inner) | copy-start | bytes 276484
  26.7 12.9 %collective-permute-start.2 = (f32[48,128]{1,0:T(8,128)S(1)}, f32[48,128]{1,0:T(8,128)S(1)}, u32[]{:S(2)}, u32[]{:S(2)}) collective-permute-start(f32[48,128]{1,0:T(8,128)S(1)} %get-tuple-element.30.refs_0_), channel_id=1, source_target_pairs={{0,24},{8,0},{16,8},{24,16},{1,25},{9,1},{17,9},{25,17},{2,26},{10... | collective-permute-start | bytes 73736 | tf_op jit(solution)/shard_map/ppermute | solution.py:558
  38.1 4.7 %collective-permute-start.1 = (f32[48,128]{1,0:T(8,128)S(1)}, f32[48,128]{1,0:T(8,128)S(1)}, u32[]{:S(2)}, u32[]{:S(2)}) collective-permute-start(f32[48,128]{1,0:T(8,128)S(1)} %get-tuple-element.30.refs_0_), channel_id=1, source_target_pairs={{0,16},{8,24},{16,0},{24,8},{1,17},{9,25},{17,1},{25,9},{2,18},{10... | collective-permute-start | bytes 73736 | tf_op jit(solution)/shard_map/ppermute | solution.py:558
  38.1 5.6 %collective-permute-start = (f32[48,128]{1,0:T(8,128)S(1)}, f32[48,128]{1,0:T(8,128)S(1)}, u32[]{:S(2)}, u32[]{:S(2)}) collective-permute-start(f32[48,128]{1,0:T(8,128)S(1)} %get-tuple-element.30.refs_0_), channel_id=1, source_target_pairs={{0,8},{8,16},{16,24},{24,0},{1,9},{9,17},{17,25},{25,1},{2,10},{10... | collective-permute-start | bytes 73736 | tf_op jit(solution)/shard_map/ppermute | solution.py:558
